TPU v7x, 32 devices: a whole 2x2x4 slice. The times are simulated.
32 devices in a mesh: grp: 2 (over y), gx: 16 (over z, x, core).
Axes of the slice: x: 2, y: 2, z: 4, core: 2. Of those that a mesh axis runs over, the one named last changes fastest.
Arguments:
- adj_final: float32 [16, 16, 64, 256], P('gx', 'grp'), parts along dimension 1, may hold values from -6 to 6
- wind_east: float32 [16, 16, 64, 256], P('gx', 'grp'), parts along dimension 1, may hold values from -0.6 to 0.6
- wind_north: float32 [16, 16, 64, 256], P('gx', 'grp'), parts along dimension 1, may hold values from -0.6 to 0.6
- relax_weight: float32 [4, 8], replicated, may hold values from 0.1 to 0.9
- rim_slot: int32 [21760], P('gx'), may hold values from 0 to 1359, as said below
Outputs:
- adj_initial: float32 [16, 16, 64, 256], P('gx', 'grp'), parts along dimension 1
- adj_rim_start: float32 [16, 21760], P('grp', 'gx'), parts along dimension 0
- adj_rim_end: float32 [16, 21760], P('grp', 'gx'), parts along dimension 0
There are 2 independent parts, one for each index of `grp`. A program takes and returns all parts, laid end to end along the dimension named above; an argument that names none is the same for every part. Nothing has to cross between parts.
Inputs may be any that keep to these rules, and one draw needn't show every extreme that they name: `rim_slot`: each aligned block of 1360 entries holds every number 0 to 1359 once.
All inputs are finite; a program needn't handle non-finite values.
Results may differ from a plain program's by a relative error of at most 0.00002.
Values sent between devices are 32-bit elements; how exact they have to be, the bound alone decides.
A program may use at most 64 MiB of HBM per device.

v0:
```python
import jax
import jax.numpy as jnp
from jax import lax
from jax.sharding import PartitionSpec as P

COL_TILES = 8
STEPS = 2
ZONE = 5


diffusion = 0.15


def shifted(shard, axis, by):
    devices = lax.axis_size(axis)
    pairs = [(i, i + by) for i in range(devices) if 0 <= i + by < devices]
    return lax.ppermute(shard, axis, pairs)


def place_pieces(pieces, offset, total, keep):
    empty = jnp.zeros((total,) + pieces.shape[1:], jnp.float32)
    return lax.dynamic_update_slice_in_dim(empty, pieces * keep, offset, 0)


def body(adj_final, wind_east, wind_north, relax_weight, rim_slot):
    adj_z = adj_final[0]
    east_wind = wind_east[0]
    north_wind = wind_north[0]
    levels, tile_r, tile_c = adj_z.shape
    tile_count = lax.axis_size("gx")
    tile_rows = tile_count // COL_TILES
    tile_index = lax.axis_index("gx")
    row_tile = tile_index // COL_TILES
    col_tile = tile_index % COL_TILES
    row_total = tile_r * tile_rows
    col_total = tile_c * COL_TILES
    local_rows = jnp.arange(tile_r, dtype=jnp.int32)
    local_cols = jnp.arange(tile_c, dtype=jnp.int32)
    row_index = row_tile * tile_r + local_rows
    column_index = col_tile * tile_c + local_cols
    row_distance = jnp.minimum(row_index, row_total - 1 - row_index)
    col_distance = jnp.minimum(column_index, col_total - 1 - column_index)
    distance = jnp.minimum(row_distance[:, None], col_distance[None, :])
    weight = jnp.where(distance == 0, 1.0, 0.0).astype(jnp.float32)[None]
    for cycle in range(1, ZONE):
        inside = jnp.where(distance == cycle, 1.0, 0.0).astype(jnp.float32)[None]
        weight = weight + inside * relax_weight[cycle - 1][:, None, None]
    row_count = (row_distance < ZONE).astype(jnp.float32)
    col_count = (col_distance < ZONE).astype(jnp.float32)
    east_coef = diffusion - 0.5 * east_wind
    west_coef = diffusion + 0.5 * east_wind
    north_coef = diffusion - 0.5 * north_wind
    south_coef = diffusion + 0.5 * north_wind
    has_left = (col_tile > 0).astype(jnp.float32)
    has_right = (col_tile < COL_TILES - 1).astype(jnp.float32)
    first_col = (local_cols == 0)[None, None, :]
    last_col = (local_cols == tile_c - 1)[None, None, :]
    first_row = (local_rows == 0)[None, :, None]
    last_row = (local_rows == tile_r - 1)[None, :, None]
    first_total = jnp.zeros(adj_z.shape, jnp.float32)
    last_total = jnp.zeros(adj_z.shape, jnp.float32)
    for step in range(STEPS, 0, -1):
        fraction = step / (STEPS + 1.0)
        target = weight * adj_z
        first_total = first_total + (1.0 - fraction) * target
        last_total = last_total + fraction * target
        adj_y = (1.0 - weight) * adj_z
        pushed = east_coef * adj_y
        pulled = west_coef * adj_y
        northward = north_coef * adj_y
        southward = south_coef * adj_y
        left_in = shifted(pushed[:, :, tile_c - 1 :], "gx", 1) * has_left
        right_in = shifted(pulled[:, :, :1], "gx", -1) * has_right
        below = shifted(northward[:, tile_r - 1 :], "gx", COL_TILES)
        above = shifted(southward[:, :1], "gx", -COL_TILES)
        from_west = jnp.where(first_col, left_in, jnp.roll(pushed, 1, axis=2))
        from_east = jnp.where(last_col, right_in, jnp.roll(pulled, -1, axis=2))
        upper_term = jnp.where(first_row, below, jnp.roll(northward, 1, axis=1))
        lower_term = jnp.where(last_row, above, jnp.roll(southward, -1, axis=1))
        adj_z = (1.0 - 4.0 * diffusion) * adj_y + from_west + from_east + upper_term + lower_term
    col_blk = col_total // tile_count
    row_blk = row_total // tile_count

    def row_strip(total, start):
        rows = lax.dynamic_slice_in_dim(total, start, ZONE, 1)
        counts = jnp.maximum(
            lax.dynamic_slice_in_dim(row_count, start, ZONE, 0)[:, None] + col_count[None, :], 1.0
        )
        return rows / counts[None]

    def col_strip(total, start):
        cols = lax.dynamic_slice_in_dim(total, start, ZONE, 2)
        counts = jnp.maximum(
            row_count[:, None] + lax.dynamic_slice_in_dim(col_count, start, ZONE, 0)[None, :], 1.0
        )
        return cols / counts[None]

    south_source = jnp.stack([row_strip(first_total, 0), row_strip(last_total, 0)])
    north_source = jnp.stack(
        [row_strip(first_total, tile_r - ZONE), row_strip(last_total, tile_r - ZONE)]
    )[:, :, ::-1, :]
    west_source = jnp.transpose(
        jnp.stack([col_strip(first_total, 0), col_strip(last_total, 0)]), (0, 1, 3, 2)
    )
    east_source = jnp.transpose(
        jnp.stack([col_strip(first_total, tile_c - ZONE), col_strip(last_total, tile_c - ZONE)])[
            :, :, :, ::-1
        ],
        (0, 1, 3, 2),
    )
    south_pieces = (
        south_source.reshape(2, levels, ZONE, tile_rows, col_blk)
        .transpose(3, 0, 1, 2, 4)
        .reshape(tile_rows, 2, levels, ZONE * col_blk)
    )
    north_pieces = (
        north_source.reshape(2, levels, ZONE, tile_rows, col_blk)
        .transpose(3, 0, 1, 2, 4)
        .reshape(tile_rows, 2, levels, ZONE * col_blk)
    )
    west_pieces = (
        west_source.reshape(2, levels, ZONE, COL_TILES, row_blk)
        .transpose(3, 0, 1, 2, 4)
        .reshape(COL_TILES, 2, levels, ZONE * row_blk)
    )
    east_pieces = (
        east_source.reshape(2, levels, ZONE, COL_TILES, row_blk)
        .transpose(3, 0, 1, 2, 4)
        .reshape(COL_TILES, 2, levels, ZONE * row_blk)
    )
    is_south = (row_tile == 0).astype(jnp.float32)
    is_north = (row_tile == tile_rows - 1).astype(jnp.float32)
    is_west = (col_tile == 0).astype(jnp.float32)
    is_east = (col_tile == COL_TILES - 1).astype(jnp.float32)
    outgoing = jnp.concatenate(
        [
            place_pieces(south_pieces, col_tile * tile_rows, tile_count, is_south),
            place_pieces(north_pieces, col_tile * tile_rows, tile_count, is_north),
            place_pieces(west_pieces, row_tile * COL_TILES, tile_count, is_west),
            place_pieces(east_pieces, row_tile * COL_TILES, tile_count, is_east),
        ],
        axis=3,
    )
    arrived = lax.all_to_all(outgoing, "gx", split_axis=0, concat_axis=0, tiled=True)
    points = arrived.sum(axis=0)
    ordered = jnp.take(points, rim_slot, axis=2)
    return (adj_z[None], ordered[0], ordered[1])


def solution(mesh):
    return jax.shard_map(
        body,
        mesh=mesh,
        in_specs=(
            P("gx", "grp", None, None),
            P("gx", "grp", None, None),
            P("gx", "grp", None, None),
            P(),
            P("gx"),
        ),
        out_specs=(P("gx", "grp", None, None), P("grp", "gx"), P("grp", "gx")),
        check_vma=False,
    )
```

profile of v0, /device:TPU:0, one launch (start us, length us, event | category | flops | bytes accessed | tf_op | source)
XLA Modules:
  0.0 154.1 jit_solution(10625488926776621367)
XLA Ops:
  1.7 0.8 slice_bitcast_fusion.7
  2.6 1.5 copy.234
  4.6 1.4 copy.235
  7.5 1.7 %bitcast_multiply_fusion.5 = (f32[8,64,256]{1,0,2:T(8,128)}, f32[8,64,256]{1,0,2:T(8,128)}, f32[8,64,256]{1,0,2:T(8,128)S(1)}) fusion(f32[8,64,256]{1,0,2:T(8,128)S(1)} %get-tuple-element.30, f32[1,8,64,256]{2,1,3,0:T(8,128)S(1)} %copy-done.8, f32[1,8,64,256]{2,1,3,0:T(8,128)S(1)} %copy.237), kind=kLoop, calls=%fused_computation.41 | loop fusion | flops 1048576 | bytes 3145728 | tf_op jit(solution)/shard_map/mul | solution.py:69
  9.2 1.0 copy-done.5
  10.2 1.4 slice.110
  11.6 1.5 copy.238
  13.1 6.5 %collective-permute-start.2 = (f32[8,1,256]{2,0,1:T(8,128)S(1)}, f32[8,1,256]{2,0,1:T(8,128)}, u32[]{:S(2)}, u32[]{:S(2)}) collective-permute-start(f32[8,1,256]{2,0,1:T(8,128)S(1)} %copy.238), channel_id=1, source_target_pairs={{0,8},{1,9},{2,10},{3,11},{4,12},{5,13},{6,14},{7,15},{16,24},{17,... | collective-permute-start | bytes 24584 | tf_op jit(solution)/shard_map/ppermute | solution.py:17
  19.6 1.3 fusion.38
  20.9 1.3 collective-permute-start.1
  22.2 1.3 fusion.35
  23.5 3.6 %collective-permute-start = (f32[8,64,1]{1,0,2:T(8,128)}, f32[8,64,1]{1,0,2:T(8,128)}, u32[]{:S(2)}, u32[]{:S(2)}) collective-permute-start(f32[8,64,1]{1,0,2:T(8,128)} %get-tuple-element.54), channel_id=1, source_target_pairs={{0,1},{1,2},{2,3},{3,4},{4,5},{5,6},{6,7},{7,8},{8,9},{9,10},{10,1... | collective-permute-start | bytes 6152 | tf_op jit(solution)/shard_map/ppermute | solution.py:17
  27.1 1.0 copy.242
  28.1 1.4 collective-permute-start.3
  29.5 3.7 %fusion.39 = (f32[8,63,256]{1,0,2:T(8,128)}, f32[1,8,63,256]{2,1,3,0:T(8,128)}, f32[1,8,63,256]{2,1,3,0:T(8,128)}, f32[8,63,256]{1,0,2:T(8,128)}) fusion(f32[8,64,256]{1,0,2:T(8,128)} %copy-done.5, f32[8,64,256]{1,0,2:T(8,128)S(1)} %get-tuple-element.29), kind=kLoop, calls=%fused_computation.124 | loop fusion | bytes 3096576 | tf_op jit(solution)/shard_map/jit(_roll_static)/slice | solution.py:78
  33.2 2.1 %fusion.36 = (f32[8,64,255]{1,0,2:T(8,128)}, f32[1,8,64,255]{2,1,3,0:T(8,128)}, f32[1,8,64,255]{2,1,3,0:T(8,128)}, f32[8,64,255]{1,0,2:T(8,128)}) fusion(f32[8,64,256]{1,0,2:T(8,128)S(1)} %copy-done.15, f32[8,64,256]{1,0,2:T(8,128)S(1)} %copy-done.14), kind=kLoop, calls=%fused_computation.121 | loop fusion | bytes 3133440 | tf_op jit(solution)/shard_map/jit(_roll_static)/slice | solution.py:76
  39.2 1.5 copy.256
  40.7 0.8 copy.259
  41.4 1.4 copy.241
  42.8 2.0 %copy.245 = f32[1,8,1,256]{2,1,3,0:T(8,128)} copy(f32[1,8,1,256]{3,1,2,0:T(8,128)} %bitcast.20) | data formatting | bytes 16384 | tf_op jit(solution)/shard_map/jit(_roll_static)/concatenate | solution.py:79
  46.2 1.5 copy.239
  47.7 1.5 copy.243
  49.2 6.8 %multiply_add_fusion.1 = (f32[8,64,256]{1,0,2:T(8,128)S(1)}, f32[8,64,256]{1,0,2:T(8,128)S(1)}) fusion(f32[8]{0:T(128)} %copy-done.35, f32[64,256]{0,1:T(8,128)} %copy-done.19, f32[8]{0:T(128)} %copy-done.37, f32[64,256]{0,1:T(8,128)S(1)} %get-tuple-element.76, f32[8]{0:T(128)} %copy-done.33, f32[64,256]{0,1:T(8,128)S(1)} %get-tuple-element.77, ...), kind=kLoop, calls=%fused_computation.47 | loop fusion | flops 3407872 | bytes 4543232 | tf_op jit(solution)/shard_map/add | solution.py:65
  56.1 3.0 %bitcast_multiply_fusion = (f32[8,64,256]{1,0,2:T(8,128)}, f32[8,64,256]{1,0,2:T(8,128)}, f32[8,64,256]{1,0,2:T(8,128)S(1)}, f32[8,64,256]{1,0,2:T(8,128)}, f32[8,64,256]{1,0,2:T(8,128)}) fusion(f32[1,8,64,256]{2,1,3,0:T(8,128)S(1)} %copy.237, f32[8,64,256]{1,0,2:T(8,128)S(1)} %get-tuple-element.28, f32[8]{0:T(128)S(1)} %copy-done.36, ...), kind=kLoop, calls=%fused_computation.36 | loop fusion | flops 3276800 | bytes 5046400 | tf_op jit(solution)/shard_map/mul | solution.py:71
  59.2 0.7 fusion.27
  60.2 1.0 copy.272
  61.2 1.9 %mul.364 = f32[8,2,8,40]{3,2,1,0:T(8,128)} reshape(f32[8,2,8,5,8]{4,3,2,1,0:T(8,128)} %bitcast.126) | data formatting | bytes 40960 | tf_op jit(solution)/shard_map/mul | solution.py:22
  63.1 1.4 fusion.26
  64.5 1.6 %mul.355 = f32[2,8,5,8,8]{4,3,1,2,0:T(8,128)} reshape(f32[2,8,5,64]{3,1,2,0:T(8,128)} %fusion.26) | data formatting | bytes 40960 | tf_op jit(solution)/shard_map/mul | solution.py:22
  66.1 2.0 %copy.273 = f32[2,8,5,8,8]{4,2,1,0,3:T(8,128)} copy(f32[2,8,5,8,8]{4,3,1,2,0:T(8,128)} %mul.355) | data formatting | bytes 40960 | tf_op jit(solution)/shard_map/mul | solution.py:22
  68.1 1.8 %mul.357 = f32[8,2,8,40]{3,2,1,0:T(8,128)} reshape(f32[8,2,8,5,8]{4,3,2,1,0:T(8,128)} %bitcast.127) | data formatting | bytes 40960 | tf_op jit(solution)/shard_map/mul | solution.py:22
  69.9 3.7 %fusion = (f32[1,8,5,256]{2,1,3,0:T(8,128)}, f32[8,5,256]{1,0,2:T(8,128)}, f32[8,5,256]{1,0,2:T(8,128)}, f32[1,8,5,256]{2,1,3,0:T(8,128)}) fusion(f32[8,64,256]{1,0,2:T(8,128)S(1)} %copy-done.3, f32[5,256]{0,1:T(8,128)} %copy.259, f32[5,256]{0,1:T(8,128)} %copy.256, f32[8,64,256]{1,0,2:T(8,128)S(1)} %copy-done.1), kind=kLoop, calls=%fused_computation.3 | loop fusion | flops 40960 | bytes 337920 | tf_op jit(solution)/shard_map/stack | solution.py:99
  73.6 2.3 %copy.260 = f32[1,8,5,256]{3,1,2,0:T(8,128)} copy(f32[1,8,5,256]{2,1,3,0:T(8,128)} %get-tuple-element.68) | data formatting | bytes 81920 | tf_op jit(solution)/shard_map/stack | solution.py:99
  75.9 2.2 %copy.261 = f32[1,8,5,256]{3,1,2,0:T(8,128)} copy(f32[1,8,5,256]{2,1,3,0:T(8,128)} %get-tuple-element.48) | data formatting | bytes 81920 | tf_op jit(solution)/shard_map/stack | solution.py:99
  78.1 1.0 copy.257
  79.5 0.9 constant_dynamic-update-slice_fusion
  80.6 1.3 concatenate.156
  81.9 8.0 %all-to-all-start = ((f32[16,2,8,1360]{3,2,1,0:T(8,128)}), f32[16,2,8,1360]{3,2,1,0:T(8,128)}, u32[]{:S(2)}, u32[]{:S(2)}) async-start(f32[16,2,8,1360]{3,2,1,0:T(8,128)} %concatenate.156), calls=%async_computation | async-start | bytes 2883584 | tf_op jit(solution)/shard_map/all_to_all | solution.py:144
  90.7 5.3 %collective-permute-start.6 = (f32[8,1,256]{2,0,1:T(8,128)S(1)}, f32[8,1,256]{2,0,1:T(8,128)}, u32[]{:S(2)}, u32[]{:S(2)}) collective-permute-start(f32[8,1,256]{2,0,1:T(8,128)S(1)} %copy.248), channel_id=1, source_target_pairs={{0,8},{1,9},{2,10},{3,11},{4,12},{5,13},{6,14},{7,15},{16,24},{17,... | collective-permute-start | bytes 24584 | tf_op jit(solution)/shard_map/ppermute | solution.py:17
  96.0 1.3 fusion.34
  97.2 1.5 collective-permute-start.5
  98.7 1.3 fusion.33
  100.0 2.3 %slice_bitcast_fusion.2 = f32[1,8,64,255]{2,1,3,0:T(8,128)} fusion(f32[8,64,256]{1,0,2:T(8,128)} %get-tuple-element.39), kind=kLoop, calls=%fused_computation.51 | loop fusion | bytes 1044480 | tf_op jit(solution)/shard_map/jit(_roll_static)/concatenate | solution.py:77
  102.4 1.1 slice_bitcast_fusion.1
  104.0 1.3 slice_bitcast_fusion
  105.3 1.0 slice_bitcast_fusion.3
  106.3 1.3 copy.251
  107.6 1.0 copy.252
  108.6 1.4 collective-permute-start.7
  110.0 2.0 %copy.255 = f32[1,8,1,256]{2,1,3,0:T(8,128)} copy(f32[1,8,1,256]{3,1,2,0:T(8,128)} %bitcast.130) | data formatting | bytes 16384 | tf_op jit(solution)/shard_map/jit(_roll_static)/concatenate | solution.py:79
  112.1 3.0 %collective-permute-start.4 = (f32[8,64,1]{1,0,2:T(8,128)}, f32[8,64,1]{1,0,2:T(8,128)S(1)}, u32[]{:S(2)}, u32[]{:S(2)}) collective-permute-start(f32[8,64,1]{1,0,2:T(8,128)} %get-tuple-element.50), channel_id=1, source_target_pairs={{0,1},{1,2},{2,3},{3,4},{4,5},{5,6},{6,7},{7,8},{8,9},{9,10},{10,1... | collective-permute-start | bytes 6152 | tf_op jit(solution)/shard_map/ppermute | solution.py:17
  115.1 1.3 multiply_bitcast_fusion.2
  117.0 1.5 copy.249
  118.5 7.0 %collective-permute-done.7 = f32[8,1,256]{2,0,1:T(8,128)} collective-permute-done((f32[8,1,256]{2,0,1:T(8,128)}, f32[8,1,256]{2,0,1:T(8,128)}, u32[]{:S(2)}, u32[]{:S(2)}) %collective-permute-start.7) | collective-permute-done | bytes 8224 | tf_op jit(solution)/shard_map/ppermute | solution.py:17
  125.4 1.5 copy.253
  126.9 9.1 %fusion.11 = f32[1,8,64,256]{2,1,3,0:T(8,128)} fusion(f32[1,8,64,255]{2,1,3,0:T(8,128)} %get-tuple-element.57, f32[1,8,64,1]{2,1,3,0:T(8,128)} %get-tuple-element.55, f32[1,8,64,1]{2,1,3,0:T(8,128)} %get-tuple-element.61, f32[1,8,64,255]{2,1,3,0:T(8,128)} %get-tuple-element.88, f32[1,8,63,256]{2,1,3,0:T(8,128)} %get-tuple-element.63, ...), kind=kLoop, calls=%fused_computation.20 | loop fusion | flops 4849664 | bytes 5612288 | tf_op jit(solution)/shard_map/add | solution.py:80
  136.0 2.3 %copy.266 = f32[1,8,64,256]{3,2,1,0:T(8,128)} copy(f32[1,8,64,256]{2,1,3,0:T(8,128)} %fusion.11) | data formatting | bytes 1048576
  138.3 1.4 reduce_sum.9
  139.8 2.1 %copy.265 = f32[2,8,1360]{1,0,2:T(2,128)} copy(f32[2,8,1360]{2,1,0:T(8,128)S(1)} %reduce_sum.9) | data formatting | bytes 174080 | tf_op jit(solution)/shard_map/reduce_sum | solution.py:145
  141.8 4.4 %gather_fusion = f32[1360,2,8]{2,1,0:T(2,128)S(1)} fusion(f32[2,8,1360]{1,0,2:T(2,128)} %copy.265, s32[2048]{0:T(1024)S(1)} %copy-done.27), kind=kCustom, calls=%fused_computation | custom fusion | bytes 179520 | tf_op jit(solution)/shard_map/jit(_take)/gather | solution.py:146
  146.3 5.0 %select_bitcast_fusion = f32[2,8,1360]{1,0,2:T(2,128)S(1)} fusion(f32[1360,2,8]{2,1,0:T(2,128)S(1)} %gather_fusion, pred[1360]{0:T(1024)(128)(4,1)S(1)} %copy-done.39), kind=kLoop, calls=%fused_computation.1 | loop fusion | flops 21760 | bytes 175440 | tf_op jit(solution)/shard_map/jit(_take)/select_n | solution.py:146
  151.2 1.1 fusion.32
  152.4 0.9 copy.267
  153.2 0.9 copy.268
  (124 shorter events, 10.9 us)
Async XLA Ops:
  0.6 3.5 %copy-start.21 = (f32[1,8,64,256]{3,2,1,0:T(8,128)S(1)}, f32[1,8,64,256]{3,2,1,0:T(8,128)}, u32[]{:S(2)}) copy-start(f32[1,8,64,256]{3,2,1,0:T(8,128)} %param.7) | copy-start | bytes 1572868
  2.6 3.6 %copy-start.31 = (f32[8]{0:T(128)}, f32[8]{0:T(128)S(1)}, u32[]{:S(2)}) copy-start(f32[8]{0:T(128)S(1)} %get-tuple-element.71) | copy-start | bytes 100
  2.6 3.6 %copy-start.33 = (f32[8]{0:T(128)}, f32[8]{0:T(128)S(1)}, u32[]{:S(2)}) copy-start(f32[8]{0:T(128)S(1)} %get-tuple-element.72) | copy-start | bytes 100
  2.6 3.6 %copy-start.35 = (f32[8]{0:T(128)}, f32[8]{0:T(128)S(1)}, u32[]{:S(2)}) copy-start(f32[8]{0:T(128)S(1)} %get-tuple-element.73) | copy-start | bytes 100
  2.6 3.6 %copy-start.37 = (f32[8]{0:T(128)}, f32[8]{0:T(128)S(1)}, u32[]{:S(2)}) copy-start(f32[8]{0:T(128)S(1)} %get-tuple-element.74) | copy-start | bytes 100
  2.6 2.0 %copy-start.22 = (f32[1,8,64,256]{3,2,1,0:T(8,128)S(1)}, f32[1,8,64,256]{3,2,1,0:T(8,128)}, u32[]{:S(2)}) copy-start(f32[1,8,64,256]{3,2,1,0:T(8,128)} %param.6) | copy-start | bytes 1572868
  4.6 1.4 copy-start.40
  4.6 1.4 copy-start.41
  6.1 0.7 copy-start.17
  6.1 0.7 copy-start.19
  6.2 1.3 copy-start.8
  6.9 2.3 %copy-start.4 = (f32[8,64,256]{1,0,2:T(8,128)}, f32[8,64,256]{1,0,2:T(8,128)S(1)}, u32[]{:S(2)}) copy-start(f32[8,64,256]{1,0,2:T(8,128)S(1)} %get-tuple-element.30) | copy-start | bytes 1572868
  9.2 1.0 copy-start.5
  13.1 33.1 %collective-permute-start.2 = (f32[8,1,256]{2,0,1:T(8,128)S(1)}, f32[8,1,256]{2,0,1:T(8,128)}, u32[]{:S(2)}, u32[]{:S(2)}) collective-permute-start(f32[8,1,256]{2,0,1:T(8,128)S(1)} %copy.238), channel_id=1, source_target_pairs={{0,8},{1,9},{2,10},{3,11},{4,12},{5,13},{6,14},{7,15},{16,24},{17,... | collective-permute-start | bytes 24584 | tf_op jit(solution)/shard_map/ppermute | solution.py:17
  20.9 24.0 %collective-permute-start.1 = (f32[8,64,1]{1,0,2:T(8,128)}, f32[8,64,1]{1,0,2:T(8,128)}, u32[]{:S(2)}, u32[]{:S(2)}) collective-permute-start(f32[8,64,1]{1,0,2:T(8,128)} %get-tuple-element.60), channel_id=1, source_target_pairs={{1,0},{2,1},{3,2},{4,3},{5,4},{6,5},{7,6},{8,7},{9,8},{10,9},{11,1... | collective-permute-start | bytes 6152 | tf_op jit(solution)/shard_map/ppermute | solution.py:17
  23.5 22.1 %collective-permute-start = (f32[8,64,1]{1,0,2:T(8,128)}, f32[8,64,1]{1,0,2:T(8,128)}, u32[]{:S(2)}, u32[]{:S(2)}) collective-permute-start(f32[8,64,1]{1,0,2:T(8,128)} %get-tuple-element.54), channel_id=1, source_target_pairs={{0,1},{1,2},{2,3},{3,4},{4,5},{5,6},{6,7},{7,8},{8,9},{9,10},{10,1... | collective-permute-start | bytes 6152 | tf_op jit(solution)/shard_map/ppermute | solution.py:17
  28.1 5.1 %copy-start.14 = (f32[8,64,256]{1,0,2:T(8,128)S(1)}, f32[8,64,256]{1,0,2:T(8,128)}, u32[]{:S(2)}) copy-start(f32[8,64,256]{1,0,2:T(8,128)} %get-tuple-element.35) | copy-start | bytes 1572868
  28.1 5.1 %copy-start.15 = (f32[8,64,256]{1,0,2:T(8,128)S(1)}, f32[8,64,256]{1,0,2:T(8,128)}, u32[]{:S(2)}) copy-start(f32[8,64,256]{1,0,2:T(8,128)} %get-tuple-element.36) | copy-start | bytes 1572868
  28.1 19.7 %collective-permute-start.3 = (f32[8,1,256]{2,0,1:T(8,128)}, f32[8,1,256]{2,0,1:T(8,128)}, u32[]{:S(2)}, u32[]{:S(2)}) collective-permute-start(f32[8,1,256]{2,0,1:T(8,128)} %copy.242), channel_id=1, source_target_pairs={{8,0},{9,1},{10,2},{11,3},{12,4},{13,5},{14,6},{15,7},{24,16},{25,... | collective-permute-start | bytes 24584 | tf_op jit(solution)/shard_map/ppermute | solution.py:17
  33.2 2.7 %copy-start.28 = (s32[1360]{0:T(1024)S(1)}, s32[1360]{0:T(1024)}, u32[]{:S(2)}) copy-start(s32[1360]{0:T(1024)} %param.9) | copy-start | bytes 16324
  49.2 6.8 %copy-start.9 = (f32[1,8,64,256]{2,1,3,0:T(8,128)S(1)}, f32[1,8,64,256]{2,1,3,0:T(8,128)}, u32[]{:S(2)}) copy-start(f32[1,8,64,256]{2,1,3,0:T(8,128)} %copy.235) | copy-start | bytes 1572868
  49.2 6.8 %copy-start.18 = (f32[64,256]{0,1:T(8,128)S(1)}, f32[64,256]{0,1:T(8,128)}, u32[]{:S(2)}) copy-start(f32[64,256]{0,1:T(8,128)} %copy-done.17) | copy-start | bytes 196612
  49.2 6.8 %copy-start.20 = (f32[64,256]{0,1:T(8,128)S(1)}, f32[64,256]{0,1:T(8,128)}, u32[]{:S(2)}) copy-start(f32[64,256]{0,1:T(8,128)} %copy-done.19) | copy-start | bytes 196612
  49.2 6.8 %copy-start.32 = (f32[8]{0:T(128)S(1)}, f32[8]{0:T(128)}, u32[]{:S(2)}) copy-start(f32[8]{0:T(128)} %copy-done.31) | copy-start | bytes 100
  49.2 6.9 %copy-start.34 = (f32[8]{0:T(128)S(1)}, f32[8]{0:T(128)}, u32[]{:S(2)}) copy-start(f32[8]{0:T(128)} %copy-done.33) | copy-start | bytes 100
  49.2 6.9 %copy-start.36 = (f32[8]{0:T(128)S(1)}, f32[8]{0:T(128)}, u32[]{:S(2)}) copy-start(f32[8]{0:T(128)} %copy-done.35) | copy-start | bytes 100
  49.2 6.9 %copy-start.38 = (f32[8]{0:T(128)S(1)}, f32[8]{0:T(128)}, u32[]{:S(2)}) copy-start(f32[8]{0:T(128)} %copy-done.37) | copy-start | bytes 100
  56.0 3.1 %copy-start = (f32[8,64,256]{1,0,2:T(8,128)}, f32[8,64,256]{1,0,2:T(8,128)S(1)}, u32[]{:S(2)}) copy-start(f32[8,64,256]{1,0,2:T(8,128)S(1)} %get-tuple-element.27) | copy-start | bytes 1572868
  56.1 3.1 %copy-start.29 = (f32[64,5]{0,1:T(8,128)S(1)}, f32[64,5]{0,1:T(8,128)}, u32[]{:S(2)}) copy-start(f32[64,5]{0,1:T(8,128)} %get-tuple-element.84) | copy-start | bytes 3844
  56.1 3.0 %copy-start.30 = (f32[64,5]{0,1:T(8,128)S(1)}, f32[64,5]{0,1:T(8,128)}, u32[]{:S(2)}) copy-start(f32[64,5]{0,1:T(8,128)} %get-tuple-element.85) | copy-start | bytes 3844
  59.1 1.0 copy-start.2
  61.2 8.7 %copy-start.1 = (f32[8,64,256]{1,0,2:T(8,128)S(1)}, f32[8,64,256]{1,0,2:T(8,128)}, u32[]{:S(2)}) copy-start(f32[8,64,256]{1,0,2:T(8,128)} %copy-done) | copy-start | bytes 1572868
  61.2 8.7 %copy-start.3 = (f32[8,64,256]{1,0,2:T(8,128)S(1)}, f32[8,64,256]{1,0,2:T(8,128)}, u32[]{:S(2)}) copy-start(f32[8,64,256]{1,0,2:T(8,128)} %copy-done.2) | copy-start | bytes 1572868
  73.6 4.5 %copy-start.13 = (f32[8,5,256]{1,0,2:T(8,128)S(1)}, f32[8,5,256]{1,0,2:T(8,128)}, u32[]{:S(2)}) copy-start(f32[8,5,256]{1,0,2:T(8,128)} %get-tuple-element.67) | copy-start | bytes 122884
  73.6 5.5 %copy-start.12 = (f32[8,5,256]{1,0,2:T(8,128)S(1)}, f32[8,5,256]{1,0,2:T(8,128)}, u32[]{:S(2)}) copy-start(f32[8,5,256]{1,0,2:T(8,128)} %get-tuple-element.49) | copy-start | bytes 122884
  79.1 1.3 copy-start.23
  79.1 1.3 copy-start.25
  79.1 1.3 copy-start.26
  79.1 1.5 copy-start.24
  81.9 8.1 %copy-start.7 = (f32[8,64,256]{1,0,2:T(8,128)S(1)}, f32[8,64,256]{1,0,2:T(8,128)}, u32[]{:S(2)}) copy-start(f32[8,64,256]{1,0,2:T(8,128)} %get-tuple-element.32) | copy-start | bytes 1572868
  81.9 56.4 %all-to-all-start = ((f32[16,2,8,1360]{3,2,1,0:T(8,128)}), f32[16,2,8,1360]{3,2,1,0:T(8,128)}, u32[]{:S(2)}, u32[]{:S(2)}) async-start(f32[16,2,8,1360]{3,2,1,0:T(8,128)} %concatenate.156), calls=%async_computation | async-start | bytes 2883584 | tf_op jit(solution)/shard_map/all_to_all | solution.py:144
  90.7 26.3 %collective-permute-start.6 = (f32[8,1,256]{2,0,1:T(8,128)S(1)}, f32[8,1,256]{2,0,1:T(8,128)}, u32[]{:S(2)}, u32[]{:S(2)}) collective-permute-start(f32[8,1,256]{2,0,1:T(8,128)S(1)} %copy.248), channel_id=1, source_target_pairs={{0,8},{1,9},{2,10},{3,11},{4,12},{5,13},{6,14},{7,15},{16,24},{17,... | collective-permute-start | bytes 24584 | tf_op jit(solution)/shard_map/ppermute | solution.py:17
  97.2 17.9 %collective-permute-start.5 = (f32[8,64,1]{1,0,2:T(8,128)}, f32[8,64,1]{1,0,2:T(8,128)}, u32[]{:S(2)}, u32[]{:S(2)}) collective-permute-start(f32[8,64,1]{1,0,2:T(8,128)} %get-tuple-element.52), channel_id=1, source_target_pairs={{1,0},{2,1},{3,2},{4,3},{5,4},{6,5},{7,6},{8,7},{9,8},{10,9},{11,1... | collective-permute-start | bytes 6152 | tf_op jit(solution)/shard_map/ppermute | solution.py:17
  102.4 1.6 %copy-start.6 = (f32[8,64,256]{1,0,2:T(8,128)S(1)}, f32[8,64,256]{1,0,2:T(8,128)}, u32[]{:S(2)}) copy-start(f32[8,64,256]{1,0,2:T(8,128)} %get-tuple-element.31) | copy-start | bytes 1572868
  103.5 1.8 %copy-start.16 = (f32[8,64,256]{1,0,2:T(8,128)S(1)}, f32[8,64,256]{1,0,2:T(8,128)}, u32[]{:S(2)}) copy-start(f32[8,64,256]{1,0,2:T(8,128)} %get-tuple-element.38) | copy-start | bytes 1572868
  107.6 19.3 %copy-start.10 = (f32[1,8,1,256]{2,1,3,0:T(8,128)S(1)}, f32[1,8,1,256]{2,1,3,0:T(8,128)}, u32[]{:S(2)}) copy-start(f32[1,8,1,256]{2,1,3,0:T(8,128)} %copy.241) | copy-start | bytes 24580
  108.6 18.3 %copy-start.11 = (f32[1,8,1,256]{2,1,3,0:T(8,128)S(1)}, f32[1,8,1,256]{2,1,3,0:T(8,128)}, u32[]{:S(2)}) copy-start(f32[1,8,1,256]{2,1,3,0:T(8,128)} %copy.245) | copy-start | bytes 24580
  108.6 16.8 %collective-permute-start.7 = (f32[8,1,256]{2,0,1:T(8,128)}, f32[8,1,256]{2,0,1:T(8,128)}, u32[]{:S(2)}, u32[]{:S(2)}) collective-permute-start(f32[8,1,256]{2,0,1:T(8,128)} %copy.252), channel_id=1, source_target_pairs={{8,0},{9,1},{10,2},{11,3},{12,4},{13,5},{14,6},{15,7},{24,16},{25,... | collective-permute-start | bytes 24584 | tf_op jit(solution)/shard_map/ppermute | solution.py:17
  112.1 4.3 %collective-permute-start.4 = (f32[8,64,1]{1,0,2:T(8,128)}, f32[8,64,1]{1,0,2:T(8,128)S(1)}, u32[]{:S(2)}, u32[]{:S(2)}) collective-permute-start(f32[8,64,1]{1,0,2:T(8,128)} %get-tuple-element.50), channel_id=1, source_target_pairs={{0,1},{1,2},{2,3},{3,4},{4,5},{5,6},{6,7},{7,8},{8,9},{9,10},{10,1... | collective-permute-start | bytes 6152 | tf_op jit(solution)/shard_map/ppermute | solution.py:17
  138.3 3.5 %copy-start.27 = (s32[2048]{0:T(1024)S(1)}, s32[2048]{0:T(1024)}, u32[]{:S(2)}) copy-start(s32[2048]{0:T(1024)} %pad_clamp_fusion) | copy-start | bytes 24580
  138.3 7.9 %copy-start.39 = (pred[1360]{0:T(1024)(128)(4,1)S(1)}, pred[1360]{0:T(1024)(128)(4,1)}, u32[]{:S(2)}) copy-start(pred[1360]{0:T(1024)(128)(4,1)} %compare_and_fusion) | copy-start | bytes 4084
where the time goes:
time: 157 us; the launch traced here: 154 us
  local copies, waits for them, and re-layouts  72.4 us (46%)
  other arithmetic  41.4 us (26%)
  starting transfers between devices  32.1 us (20%)
  waiting for transfers between devices  7 us (4%)
    ppermute x8, starting transfers between devices, shifted(): return lax.ppermute(shard, axis, pairs)  24 us
    unnamed x90, local copies, waits for them, and re-layouts  9.85 us
    add x1, other arithmetic, body(): (1.0 - 4.0 * diffusion) * adj_y + from_west + from_east + upper_term  9.06 us
    mul x6, local copies, waits for them, and re-layouts, place_pieces(): return lax.dynamic_update_slice_in_dim(empty, pieces * keep, offset, 0)  8.49 us
    all_to_all x1, starting transfers between devices, body(): lax.all_to_all(outgoing, 'gx', split_axis=0, concat_axis=0, tiled=True)  8.04 us
    ppermute x8, waiting for transfers between devices, shifted(): return lax.ppermute(shard, axis, pairs)  7 us
    add x1, other arithmetic, body(): first_total = first_total + (1.0 - fraction) * target  6.76 us
    concatenate x3, local copies, waits for them, and re-layouts, body(): lower_term = jnp.where(last_row, above, jnp.roll(southward, -1, axis=1))  5.36 us
  transfers between devices with their start and end apart: 9, of which 1 were waited for; matrix products, arithmetic and copies ran while one was open for 33% of the time, Pallas kernels for 0%

commit v1 on v0

v1 whole, which is shorter than its diff:
```python
import functools

import jax
import jax.numpy as jnp
from jax import lax
from jax.experimental import pallas as pl
from jax.experimental.pallas import tpu as pltpu
from jax.sharding import PartitionSpec as P

COL_TILES = 8
STEPS = 2
ZONE = 5
LANES = 128

diffusion = 0.15


def iota(shape, axis):
    return lax.broadcasted_iota(jnp.int32, shape, axis)


def adjoint_kernel(tile_rows, cb, z_hbm, e_hbm, n_hbm, relax, out, pts,
                   z, e, n, omw, z1, send_col, recv_col, send_row, recv_row,
                   strip, row_out, col_out, row_in, col_in,
                   in_sem, hs_sem, hr_sem, rs_sem, rr_sem, cs_sem, cr_sem):
    levels, tile_r, tile_c = z.shape
    row_blk = tile_r // COL_TILES
    me = lax.axis_index("gx")
    ti = lax.div(me, COL_TILES)
    tj = lax.rem(me, COL_TILES)
    south, north = ti == 0, ti == tile_rows - 1
    west, east = tj == 0, tj == COL_TILES - 1

    loads = [pltpu.make_async_copy(src.at[0], dst, in_sem.at[k])
             for k, (src, dst) in enumerate([(z_hbm, z), (e_hbm, e), (n_hbm, n)])]
    for load in loads:
        load.start()

    ways = [
        (~east, me + 1, ~west, me - 1),
        (~west, me - 1, ~east, me + 1),
        (~north, me + COL_TILES, ~south, me - COL_TILES),
        (~south, me - COL_TILES, ~north, me + COL_TILES),
    ]
    row_source = [lax.div(me, tile_rows), (tile_rows - 1) * COL_TILES + lax.div(me, tile_rows)]
    col_source = [ti * COL_TILES, ti * COL_TILES + COL_TILES - 1]

    barrier = pltpu.get_barrier_semaphore()

    def greet(cond, who):
        @pl.when(cond)
        def _():
            pl.semaphore_signal(barrier, inc=1, device_id={"gx": who},
                                device_id_type=pl.DeviceIdType.MESH)

    for sends, target, receives, source in ways:
        greet(receives, source)
    for source in row_source + col_source:
        greet(source != me, source)

    for d in range(2):
        @pl.when(~ways[d][2])
        def _(d=d):
            for step in range(STEPS):
                recv_col[step, d] = jnp.zeros((tile_r, LANES), jnp.float32)

        @pl.when(~ways[2 + d][2])
        def _(d=d):
            for step in range(STEPS):
                recv_row[step, d] = jnp.zeros((levels, tile_c), jnp.float32)

    row_total, col_total = tile_r * tile_rows, tile_c * COL_TILES
    rows = ti * tile_r + iota((tile_r, tile_c), 0)
    cols = tj * tile_c + iota((tile_r, tile_c), 1)
    distance = jnp.minimum(jnp.minimum(rows, row_total - 1 - rows),
                           jnp.minimum(cols, col_total - 1 - cols))
    for l in range(levels):
        value = jnp.where(distance == 0, 0.0, 1.0)
        for cycle in range(1, ZONE):
            value = jnp.where(distance == cycle, 1.0 - relax[cycle - 1, l], value)
        omw[l] = value

    row_sends = jnp.where(south | north, tile_rows, 0)
    col_sends = jnp.where(west | east, COL_TILES, 0)
    total = row_sends + col_sends
    for sends, _, _, _ in ways:
        total = total + jnp.where(sends, 1, 0)
    row_base, col_base = tj * tile_rows, ti * COL_TILES
    own_row = (south | north) & (me >= row_base) & (me < row_base + tile_rows)
    own_col = west | east
    total = total - jnp.where(own_row, 1, 0) - jnp.where(own_col, 1, 0)

    for load in loads:
        load.wait()
    pl.semaphore_wait(barrier, total)

    lane = iota((tile_r, LANES), 1)
    lane_w = iota((tile_r, tile_c), 1)
    row_w = iota((tile_r, tile_c), 0)

    def halo(step, d):
        sends, target, receives, source = ways[d]
        if d < 2:
            src, dst = send_col.at[step, d], recv_col.at[step, d]
        else:
            src, dst = send_row.at[step, d - 2], recv_row.at[step, d - 2]
        return pltpu.make_async_remote_copy(
            src_ref=src, dst_ref=dst, send_sem=hs_sem.at[step, d], recv_sem=hr_sem.at[step, d],
            device_id={"gx": jnp.where(sends, target, source)},
            device_id_type=pl.DeviceIdType.MESH)

    def apply(source, dest, step):
        packs = [jnp.zeros((tile_r, LANES), jnp.float32)] * 2
        for l in range(levels):
            y = omw[l] * source[l]
            ew, nw = 0.5 * e[l], 0.5 * n[l]
            dy = diffusion * y
            ey, ny = ew * y, nw * y
            pushed = pltpu.roll(dy - ey, 1, 1)
            pulled = pltpu.roll(dy + ey, tile_c - 1, 1)
            northward, southward = dy - ny, dy + ny
            send_row[step, 0, l:l + 1, :] = northward[tile_r - 1:tile_r]
            send_row[step, 1, l:l + 1, :] = southward[0:1]
            up = pltpu.roll(northward, 1, 0)
            down = pltpu.roll(southward, tile_r - 1, 0)
            first, last = pushed[:, :LANES], pulled[:, tile_c - LANES:]
            packs[0] = jnp.where(lane == l, pltpu.roll(first, l, 1) if l else first, packs[0])
            packs[1] = jnp.where(lane == l, pltpu.roll(last, l + 1, 1), packs[1])
            dest[l] = ((1.0 - 4.0 * diffusion) * y
                       + jnp.where(lane_w == 0, 0.0, pushed)
                       + jnp.where(lane_w == tile_c - 1, 0.0, pulled)
                       + jnp.where(row_w == 0, 0.0, up)
                       + jnp.where(row_w == tile_r - 1, 0.0, down))
        for d in range(2):
            send_col[step, d] = packs[d]
        for d in range(4):
            @pl.when(ways[d][0])
            def _(d=d):
                halo(step, d).start()

    def finish(dest, step):
        for d in range(4):
            @pl.when(ways[d][2])
            def _(d=d):
                halo(step, d).wait_recv()
        left, right = recv_col[step, 0], recv_col[step, 1]
        for l in range(levels):
            moved = pltpu.roll(left, LANES - l, 1) if l else left
            dest[l, :, :LANES] = dest[l, :, :LANES] + jnp.where(lane == 0, moved, 0.0)
            moved = pltpu.roll(right, LANES - 1 - l, 1)
            dest[l, :, tile_c - LANES:] = dest[l, :, tile_c - LANES:] + jnp.where(
                lane == LANES - 1, moved, 0.0)
            dest[l, 0:1, :] = dest[l, 0:1, :] + recv_row[step, 0, l:l + 1, :]
            dest[l, tile_r - 1:tile_r, :] = (
                dest[l, tile_r - 1:tile_r, :] + recv_row[step, 1, l:l + 1, :])

    apply(z, z1, 0)
    finish(z1, 0)

    def two(t2, t1):
        one, third = 2.0 / (STEPS + 1.0), 1.0 / (STEPS + 1.0)
        return (1.0 - one) * t2 + (1.0 - third) * t1, one * t2 + third * t1

    lane_p = iota((2 * levels, LANES), 1)
    lane_l = iota((levels, LANES), 1)

    def piece(out_ref, in_ref, k, slot, s_sem, r_sem, target):
        return pltpu.make_async_remote_copy(
            src_ref=out_ref.at[k], dst_ref=in_ref.at[slot], send_sem=s_sem.at[k],
            recv_sem=r_sem.at[slot], device_id={"gx": target},
            device_id_type=pl.DeviceIdType.MESH)

    def each_piece(out_ref, in_ref, count, base, slots, s_sem, r_sem, start):
        for slot, cond in enumerate(slots):
            for k in range(count):
                target = base + k

                @pl.when(cond & (target != me))
                def _():
                    copy = piece(out_ref, in_ref, k, slot, s_sem, r_sem, target)
                    if start:
                        copy.start()
                    else:
                        copy.wait_send()

                if start:
                    @pl.when(cond & (target == me))
                    def _():
                        in_ref[slot] = out_ref[k]

    row_args = (row_out, row_in, tile_rows, row_base, (south, north), rs_sem, rr_sem)
    col_args = (col_out, col_in, COL_TILES, col_base, (west, east), cs_sem, cr_sem)

    @pl.when(south | north)
    def _():
        col_index = tj * tile_c + iota((levels, tile_c), 1)
        inverse = jnp.where(jnp.minimum(col_index, col_total - 1 - col_index) < ZONE, 0.5, 1.0)
        for w in range(ZONE):
            def pick(ref):
                return jnp.where(north, ref[:, tile_r - 1 - w, :], ref[:, w, :])
            weight = (1.0 - pick(omw)) * inverse
            values = jnp.concatenate(two(weight * pick(z), weight * pick(z1)), axis=0)
            for t in range(tile_rows):
                if cb % LANES == 0:
                    row_out[t, :, w * cb:(w + 1) * cb] = values[:, t * cb:(t + 1) * cb]
                    continue
                block, offset = divmod(w * cb, LANES)
                from_block, from_offset = divmod(t * cb, LANES)
                shift = (offset - from_offset) % LANES
                part = values[:, from_block * LANES:(from_block + 1) * LANES]
                part = pltpu.roll(part, shift, 1) if shift else part
                there = slice(block * LANES, (block + 1) * LANES)
                if offset:
                    part = jnp.where(lane_p >= offset, part, row_out[t, :, there])
                row_out[t, :, there] = part
        each_piece(*row_args, True)

    @pl.when(west | east)
    def _():
        row_index = ti * tile_r + iota((tile_r, LANES), 0)
        inverse = jnp.where(jnp.minimum(row_index, row_total - 1 - row_index) < ZONE, 0.5, 1.0)
        for l in range(levels):
            def pick(ref):
                return jnp.where(east, ref[l, :, tile_c - LANES:], ref[l, :, :LANES])
            weight = (1.0 - pick(omw)) * inverse
            values = jnp.concatenate(two(weight * pick(z), weight * pick(z1)), axis=0)
            turned = jnp.transpose(values)
            strip[:, l, :] = jnp.where(east, turned[LANES - 8:], turned[:8])
        lines = [jnp.where(east, strip[7 - w], strip[w]) for w in range(ZONE)]
        for k in range(COL_TILES):
            for f in range(2):
                value = jnp.zeros((levels, LANES), jnp.float32)
                for w in range(ZONE):
                    shift = (w * row_blk - f * tile_r - k * row_blk) % LANES
                    moved = pltpu.roll(lines[w], shift, 1) if shift else lines[w]
                    inside = (lane_l >= w * row_blk) & (lane_l < (w + 1) * row_blk)
                    value = jnp.where(inside, moved, value)
                col_out[k, f * levels:(f + 1) * levels, :] = value
        each_piece(*col_args, True)

    apply(z1, out, 1)
    finish(out, 1)

    for slot in range(2):
        @pl.when(row_source[slot] != me)
        def _(slot=slot):
            piece(row_out, row_in, 0, slot, rs_sem, rr_sem, row_source[slot]).wait_recv()

        @pl.when(col_source[slot] != me)
        def _(slot=slot):
            piece(col_out, col_in, 0, slot, cs_sem, cr_sem, col_source[slot]).wait_recv()

    width = row_in.shape[2]
    side = ZONE * row_blk
    pts[:, :width] = row_in[0]
    pts[:, width:2 * width] = row_in[1]
    pts[:, 2 * width:] = jnp.where(lane_p < side, col_in[0], pltpu.roll(col_in[1], side, 1))

    for step in range(STEPS):
        for d in range(4):
            @pl.when(ways[d][0])
            def _(step=step, d=d):
                halo(step, d).wait_send()
    each_piece(*row_args, False)
    each_piece(*col_args, False)


def order_kernel(cb, width, pts, slot_ref, first_out, last_out, index):
    levels, rim_blk = first_out.shape
    span = ZONE * cb
    blocks = pts.shape[1] // LANES
    index[...] = jnp.zeros(index.shape, jnp.int32)
    index[:, :rim_blk] = jnp.broadcast_to(slot_ref[...], (2 * levels, rim_blk))
    for s in range(0, rim_blk, LANES):
        q = index[:, s:s + LANES]
        place = jnp.where(q < span, q, jnp.where(q < 2 * span, q + (width - span),
                                                 q + 2 * (width - span)))
        high, low = place // LANES, place % LANES
        total = jnp.zeros((2 * levels, LANES), jnp.float32)
        for b in range(blocks):
            found = jnp.take_along_axis(pts[:, b * LANES:(b + 1) * LANES], low, axis=1)
            total = jnp.where(high == b, found, total)
        size = min(LANES, rim_blk - s)
        first_out[:, s:s + size] = total[:levels, :size]
        last_out[:, s:s + size] = total[levels:, :size]


def body(adj_final, wind_east, wind_north, relax_weight, rim_slot):
    _, levels, tile_r, tile_c = adj_final.shape
    tile_count = lax.axis_size("gx")
    tile_rows = tile_count // COL_TILES
    cb = tile_c // tile_rows
    width = -(-ZONE * cb // LANES) * LANES
    f32 = jnp.float32
    field = pltpu.VMEM((levels, tile_r, tile_c), f32)
    dma = pltpu.SemaphoreType.DMA
    vmem, anywhere = pl.BlockSpec(memory_space=pltpu.VMEM), pl.BlockSpec(memory_space=pl.ANY)
    total = 2 * width + LANES
    adj, pts = pl.pallas_call(
        functools.partial(adjoint_kernel, tile_rows, cb),
        out_shape=(jax.ShapeDtypeStruct((levels, tile_r, tile_c), f32),
                   jax.ShapeDtypeStruct((2 * levels, total), f32)),
        in_specs=[anywhere] * 3 + [pl.BlockSpec(memory_space=pltpu.SMEM)],
        out_specs=(vmem, vmem),
        scratch_shapes=[
            field, field, field, field, field,
            pltpu.VMEM((STEPS, 2, tile_r, LANES), f32),
            pltpu.VMEM((STEPS, 2, tile_r, LANES), f32),
            pltpu.VMEM((STEPS, 2, levels, tile_c), f32),
            pltpu.VMEM((STEPS, 2, levels, tile_c), f32),
            pltpu.VMEM((8, levels, LANES), f32),
            pltpu.VMEM((tile_rows, 2 * levels, width), f32),
            pltpu.VMEM((COL_TILES, 2 * levels, LANES), f32),
            pltpu.VMEM((2, 2 * levels, width), f32),
            pltpu.VMEM((2, 2 * levels, LANES), f32),
            dma((3,)), dma((STEPS, 4)), dma((STEPS, 4)),
            dma((tile_rows,)), dma((2,)), dma((COL_TILES,)), dma((2,)),
        ],
        compiler_params=pltpu.CompilerParams(
            collective_id=0, has_side_effects=True, vmem_limit_bytes=32 * 1024 * 1024),
        cost_estimate=pl.CostEstimate(flops=10_000_000, bytes_accessed=2_200_000,
                                      transcendentals=0),
    )(adj_final, wind_east, wind_north, relax_weight)
    rim_blk = rim_slot.shape[0]
    padded = -(-rim_blk // LANES) * LANES
    first, last = pl.pallas_call(
        functools.partial(order_kernel, cb, width),
        out_shape=(jax.ShapeDtypeStruct((levels, rim_blk), f32),) * 2,
        in_specs=[vmem, vmem],
        out_specs=(vmem, vmem),
        scratch_shapes=[pltpu.VMEM((2 * levels, padded), jnp.int32)],
    )(pts, rim_slot.reshape(1, rim_blk))
    return (adj[None], first, last)


def solution(mesh):
    return jax.shard_map(
        body,
        mesh=mesh,
        in_specs=(
            P("gx", "grp", None, None),
            P("gx", "grp", None, None),
            P("gx", "grp", None, None),
            P(),
            P("gx"),
        ),
        out_specs=(P("gx", "grp", None, None), P("grp", "gx"), P("grp", "gx")),
        check_vma=False,
    )
```

time: 157 us -> 22.9 us (0.15); the launches traced: 154 us -> 22.6 us
  local copies, waits for them, and re-layouts: 72.4 us -> 5.82 us
  other arithmetic: 41.4 us -> 0 us
  starting transfers between devices: 32.1 us -> 0 us
  Pallas kernels: 0 us -> 16.2 us
  waiting for transfers between devices: 7 us -> 0 us
    ppermute x8 -> x0, starting transfers between devices: 24 us -> none  [shifted(): return lax.ppermute(shard, axis, pairs)]
    slice x13 -> x0, local copies, waits for them, and re-layouts: 17.7 us -> none  [the longest x1 3.7 us: body(): upper_term = jnp.where(first_row, below, jnp.roll(northward, 1, axis=1))]
    pallas_call x0 -> x2, Pallas kernels: none -> 16.2 us  [the longest x1 14 us: body(): pl.pallas_call(functools.partial(adjoint_kernel, tile_rows, cb), out_shap...]
    add x2 -> x0, other arithmetic: 15.8 us -> none  [the longest x1 9.06 us: body(): (1.0 - 4.0 * diffusion) * adj_y + from_west + from_east + upper_term]
    concatenate x9 -> x0, local copies, waits for them, and re-layouts: 13.9 us -> none  [the longest x3 5.36 us: body(): lower_term = jnp.where(last_row, above, jnp.roll(southward, -1, axis=1))]
    mul x7 -> x0, local copies, waits for them, and re-layouts: 9.32 us -> none  [the longest x6 8.49 us: place_pieces(): return lax.dynamic_update_slice_in_dim(empty, pieces * keep, offset, 0)]
    all_to_all x1 -> x0, starting transfers between devices: 8.04 us -> none  [body(): lax.all_to_all(outgoing, 'gx', split_axis=0, concat_axis=0, tiled=True)]
    ppermute x8 -> x0, waiting for transfers between devices: 7 us -> none  [shifted(): return lax.ppermute(shard, axis, pairs)]
  transfers between devices with their start and end apart: 9 -> 0, of which waited for: 1 -> 0; matrix products, arithmetic and copies ran while one was open for 33% -> 0% of each run, Pallas kernels for 0% -> 0%
where the time goes in v1:
time: 22.9 us; the launch traced here: 22.6 us
  Pallas kernels  16.2 us (71%)
  local copies, waits for them, and re-layouts  5.82 us (25%)
  between operations  0.66 us (3%)
    pallas_call x1, Pallas kernels, body(): pl.pallas_call(functools.partial(adjoint_kernel, tile_rows, cb), out_shap...  14 us
    unnamed x13, local copies, waits for them, and re-layouts  5.23 us
    pallas_call x1, Pallas kernels, body(): pl.pallas_call(functools.partial(order_kernel, cb, width), out_shape=(jax...  2.1 us
    reshape x1, local copies, waits for them, and re-layouts, body(): rim_slot.reshape(1, rim_blk)  0.59 us

profile of v1, /device:TPU:0, one launch (start us, length us, event | category | flops | bytes accessed | tf_op | source)
XLA Modules:
  0.0 22.6 jit_solution(16698166838290620594)
XLA Ops:
  0.6 0.0 copy-start
  0.6 1.0 %copy-done = f32[1,8,64,256]{3,2,1,0:T(8,128)S(1)} copy-done((f32[1,8,64,256]{3,2,1,0:T(8,128)S(1)}, f32[1,8,64,256]{3,2,1,0:T(8,128)}, u32[]{:S(2)}) %copy-start) | copy-done | bytes 524312
  1.7 0.0 copy-start.1
  1.7 1.0 %copy-done.1 = f32[1,8,64,256]{3,2,1,0:T(8,128)S(1)} copy-done((f32[1,8,64,256]{3,2,1,0:T(8,128)S(1)}, f32[1,8,64,256]{3,2,1,0:T(8,128)}, u32[]{:S(2)}) %copy-start.1) | copy-done | bytes 524312
  2.7 0.0 copy-start.2
  2.7 1.0 %copy-done.2 = f32[1,8,64,256]{3,2,1,0:T(8,128)S(1)} copy-done((f32[1,8,64,256]{3,2,1,0:T(8,128)S(1)}, f32[1,8,64,256]{3,2,1,0:T(8,128)}, u32[]{:S(2)}) %copy-start.2) | copy-done | bytes 524312
  3.8 0.0 copy-start.4
  3.8 0.7 %copy-done.4 = f32[4,8]{1,0:T(4,128)S(1)} copy-done((f32[4,8]{1,0:T(4,128)S(1)}, f32[4,8]{1,0:T(4,128)}, u32[]{:S(2)}) %copy-start.4) | copy-done | bytes 152
  4.4 0.0 copy-start.5
  4.4 14.0 %shard_map.76 = (f32[8,64,256]{2,1,0:T(8,128)S(1)}, f32[16,1408]{1,0:T(8,128)S(1)}) custom-call(f32[1,8,64,256]{3,2,1,0:T(8,128)S(1)} %copy-done, f32[1,8,64,256]{3,2,1,0:T(8,128)S(1)} %copy-done.1, f32[1,8,64,256]{3,2,1,0:T(8,128)S(1)} %copy-done.2, f32[4,8]{1,0:T(4,128)S(1)} %copy-done.4), custom_call_target="tpu_custom_call" | custom-call | flops 10000000 | bytes 2200000 | tf_op jit(solution)/shard_map/pallas_call | solution.py:299
  18.5 0.0 copy-start.3
  18.5 0.6 %copy-done.3 = f32[16,1408]{1,0:T(8,128)} copy-done((f32[16,1408]{1,0:T(8,128)}, f32[16,1408]{1,0:T(8,128)S(1)}, u32[]{:S(2)}) %copy-start.3) | copy-done | bytes 90136
  19.1 0.0 copy-done.5
  19.1 0.6 %reshape.9.slot_ref = s32[1,1360]{1,0:T(1,128)} reshape(s32[1360]{0:T(1024)S(1)} %copy-done.5) | data formatting | bytes 10880 | tf_op jit(solution)/shard_map/reshape | solution.py:332
  19.7 2.1 %shard_map.77 = (f32[8,1360]{1,0:T(8,128)}, f32[8,1360]{1,0:T(8,128)}) custom-call(f32[16,1408]{1,0:T(8,128)} %copy-done.3, s32[1,1360]{1,0:T(1,128)} %reshape.9.slot_ref), custom_call_target="tpu_custom_call" | custom-call | tf_op jit(solution)/shard_map/pallas_call | solution.py:326
  21.8 0.8 %copy.9 = f32[1,8,64,256]{3,2,1,0:T(8,128)} copy(f32[1,8,64,256]{3,2,1,0:T(8,128)S(1)} %bitcast.1) | data formatting | bytes 1048576
Async XLA Ops:
  0.6 1.0 %copy-start = (f32[1,8,64,256]{3,2,1,0:T(8,128)S(1)}, f32[1,8,64,256]{3,2,1,0:T(8,128)}, u32[]{:S(2)}) copy-start(f32[1,8,64,256]{3,2,1,0:T(8,128)} %z_hbm.1) | copy-start | bytes 1572868
  1.7 1.0 %copy-start.1 = (f32[1,8,64,256]{3,2,1,0:T(8,128)S(1)}, f32[1,8,64,256]{3,2,1,0:T(8,128)}, u32[]{:S(2)}) copy-start(f32[1,8,64,256]{3,2,1,0:T(8,128)} %e_hbm.1) | copy-start | bytes 1572868
  2.7 1.0 %copy-start.2 = (f32[1,8,64,256]{3,2,1,0:T(8,128)S(1)}, f32[1,8,64,256]{3,2,1,0:T(8,128)}, u32[]{:S(2)}) copy-start(f32[1,8,64,256]{3,2,1,0:T(8,128)} %n_hbm.1) | copy-start | bytes 1572868
  3.8 0.7 %copy-start.4 = (f32[4,8]{1,0:T(4,128)S(1)}, f32[4,8]{1,0:T(4,128)}, u32[]{:S(2)}) copy-start(f32[4,8]{1,0:T(4,128)} %relax.1) | copy-start | bytes 388
  4.4 14.7 %copy-start.5 = (s32[1360]{0:T(1024)S(1)}, s32[1360]{0:T(1024)}, u32[]{:S(2)}) copy-start(s32[1360]{0:T(1024)} %param.9) | copy-start | bytes 16324
  18.5 0.6 %copy-start.3 = (f32[16,1408]{1,0:T(8,128)}, f32[16,1408]{1,0:T(8,128)S(1)}, u32[]{:S(2)}) copy-start(f32[16,1408]{1,0:T(8,128)S(1)} %get-tuple-element.8.pts) | copy-start | bytes 270340

commit v2 on v1

--- a/solution.py
+++ b/solution.py
@@ -19,10 +19,10 @@
     return lax.broadcasted_iota(jnp.int32, shape, axis)
 
 
-def adjoint_kernel(tile_rows, cb, z_hbm, e_hbm, n_hbm, relax, out, pts,
-                   z, e, n, omw, z1, send_col, recv_col, send_row, recv_row,
-                   strip, row_out, col_out, row_in, col_in,
-                   in_sem, hs_sem, hr_sem, rs_sem, rr_sem, cs_sem, cr_sem):
+def adjoint_kernel(tile_rows, cb, z_hbm, e_hbm, n_hbm, relax_hbm, out, pts,
+                   relax, z, e, n, omw, z1, send_col, recv_col, send_row, recv_row,
+                   early, strip, row_out, col_out, row_in, col_in,
+                   relax_sem, in_sem, hs_sem, hr_sem, rs_sem, rr_sem, cs_sem, cr_sem):
     levels, tile_r, tile_c = z.shape
     row_blk = tile_r // COL_TILES
     me = lax.axis_index("gx")
@@ -33,6 +33,8 @@
 
     loads = [pltpu.make_async_copy(src.at[0], dst, in_sem.at[k])
              for k, (src, dst) in enumerate([(z_hbm, z), (e_hbm, e), (n_hbm, n)])]
+    relax_load = pltpu.make_async_copy(relax_hbm, relax, relax_sem)
+    relax_load.start()
     for load in loads:
         load.start()
 
@@ -74,6 +76,7 @@
     cols = tj * tile_c + iota((tile_r, tile_c), 1)
     distance = jnp.minimum(jnp.minimum(rows, row_total - 1 - rows),
                            jnp.minimum(cols, col_total - 1 - cols))
+    relax_load.wait()
     for l in range(levels):
         value = jnp.where(distance == 0, 0.0, 1.0)
         for cycle in range(1, ZONE):
@@ -92,7 +95,6 @@
 
     for load in loads:
         load.wait()
-    pl.semaphore_wait(barrier, total)
 
     lane = iota((tile_r, LANES), 1)
     lane_w = iota((tile_r, tile_c), 1)
@@ -109,34 +111,43 @@
             device_id={"gx": jnp.where(sends, target, source)},
             device_id_type=pl.DeviceIdType.MESH)
 
-    def apply(source, dest, step):
+    def edges(source, step):
+        def weighted(place):
+            return omw[place] * source[place]
+        ends = (slice(None), tile_r - 1, slice(None)), (slice(None), 0, slice(None))
+        send_row[step, 0] = (diffusion - 0.5 * n[ends[0]]) * weighted(ends[0])
+        send_row[step, 1] = (diffusion + 0.5 * n[ends[1]]) * weighted(ends[1])
         packs = [jnp.zeros((tile_r, LANES), jnp.float32)] * 2
         for l in range(levels):
+            place = (l, slice(None), slice(tile_c - LANES, tile_c))
+            value = (diffusion - 0.5 * e[place]) * weighted(place)
+            packs[0] = jnp.where(lane == l, pltpu.roll(value, l + 1, 1), packs[0])
+            place = (l, slice(None), slice(0, LANES))
+            value = (diffusion + 0.5 * e[place]) * weighted(place)
+            packs[1] = jnp.where(lane == l, pltpu.roll(value, l, 1) if l else value, packs[1])
+        for d in range(2):
+            send_col[step, d] = packs[d]
+        if step == 0:
+            pl.semaphore_wait(barrier, total)
+        for d in range(4):
+            @pl.when(ways[d][0])
+            def _(d=d):
+                halo(step, d).start()
+
+    def interior(source, dest):
+        for l in range(levels):
             y = omw[l] * source[l]
-            ew, nw = 0.5 * e[l], 0.5 * n[l]
             dy = diffusion * y
-            ey, ny = ew * y, nw * y
+            ey, ny = 0.5 * e[l] * y, 0.5 * n[l] * y
             pushed = pltpu.roll(dy - ey, 1, 1)
             pulled = pltpu.roll(dy + ey, tile_c - 1, 1)
-            northward, southward = dy - ny, dy + ny
-            send_row[step, 0, l:l + 1, :] = northward[tile_r - 1:tile_r]
-            send_row[step, 1, l:l + 1, :] = southward[0:1]
-            up = pltpu.roll(northward, 1, 0)
-            down = pltpu.roll(southward, tile_r - 1, 0)
-            first, last = pushed[:, :LANES], pulled[:, tile_c - LANES:]
-            packs[0] = jnp.where(lane == l, pltpu.roll(first, l, 1) if l else first, packs[0])
-            packs[1] = jnp.where(lane == l, pltpu.roll(last, l + 1, 1), packs[1])
+            up = pltpu.roll(dy - ny, 1, 0)
+            down = pltpu.roll(dy + ny, tile_r - 1, 0)
             dest[l] = ((1.0 - 4.0 * diffusion) * y
                        + jnp.where(lane_w == 0, 0.0, pushed)
                        + jnp.where(lane_w == tile_c - 1, 0.0, pulled)
                        + jnp.where(row_w == 0, 0.0, up)
                        + jnp.where(row_w == tile_r - 1, 0.0, down))
-        for d in range(2):
-            send_col[step, d] = packs[d]
-        for d in range(4):
-            @pl.when(ways[d][0])
-            def _(d=d):
-                halo(step, d).start()
 
     def finish(dest, step):
         for d in range(4):
@@ -154,8 +165,32 @@
             dest[l, tile_r - 1:tile_r, :] = (
                 dest[l, tile_r - 1:tile_r, :] + recv_row[step, 1, l:l + 1, :])
 
-    apply(z, z1, 0)
+    half = levels // 2
+
+    def turned_columns(ref):
+        row_index = ti * tile_r + iota((tile_r, LANES), 0)
+        inverse = jnp.where(jnp.minimum(row_index, row_total - 1 - row_index) < ZONE, 0.5, 1.0)
+        result = []
+        for m in range(half):
+            parts = []
+            for l in (m, m + half):
+                def pick(r, l=l):
+                    return jnp.where(east, r[l, :, tile_c - LANES:], r[l, :, :LANES])
+                parts.append((1.0 - pick(omw)) * inverse * pick(ref))
+            turned = jnp.transpose(jnp.concatenate(parts, axis=0))
+            result.append(jnp.where(east, turned[LANES - 8:], turned[:8]))
+        return result
+
+    edges(z, 0)
+    interior(z, z1)
+
+    @pl.when(west | east)
+    def _():
+        for m, turned in enumerate(turned_columns(z)):
+            early[m] = turned
+
     finish(z1, 0)
+    edges(z1, 1)
 
     def two(t2, t1):
         one, third = 2.0 / (STEPS + 1.0), 1.0 / (STEPS + 1.0)
@@ -199,7 +234,8 @@
             def pick(ref):
                 return jnp.where(north, ref[:, tile_r - 1 - w, :], ref[:, w, :])
             weight = (1.0 - pick(omw)) * inverse
-            values = jnp.concatenate(two(weight * pick(z), weight * pick(z1)), axis=0)
+            first, last = two(weight * pick(z), weight * pick(z1))
+            values = jnp.concatenate([first[:half], last[:half], first[half:], last[half:]], axis=0)
             for t in range(tile_rows):
                 if cb % LANES == 0:
                     row_out[t, :, w * cb:(w + 1) * cb] = values[:, t * cb:(t + 1) * cb]
@@ -217,15 +253,10 @@
 
     @pl.when(west | east)
     def _():
-        row_index = ti * tile_r + iota((tile_r, LANES), 0)
-        inverse = jnp.where(jnp.minimum(row_index, row_total - 1 - row_index) < ZONE, 0.5, 1.0)
-        for l in range(levels):
-            def pick(ref):
-                return jnp.where(east, ref[l, :, tile_c - LANES:], ref[l, :, :LANES])
-            weight = (1.0 - pick(omw)) * inverse
-            values = jnp.concatenate(two(weight * pick(z), weight * pick(z1)), axis=0)
-            turned = jnp.transpose(values)
-            strip[:, l, :] = jnp.where(east, turned[LANES - 8:], turned[:8])
+        for m, turned in enumerate(turned_columns(z1)):
+            first, last = two(early[m], turned)
+            strip[:, m, :] = first
+            strip[:, half + m, :] = last
         lines = [jnp.where(east, strip[7 - w], strip[w]) for w in range(ZONE)]
         for k in range(COL_TILES):
             for f in range(2):
@@ -238,7 +269,7 @@
                 col_out[k, f * levels:(f + 1) * levels, :] = value
         each_piece(*col_args, True)
 
-    apply(z1, out, 1)
+    interior(z1, out)
     finish(out, 1)
 
     for slot in range(2):
@@ -265,14 +296,18 @@
     each_piece(*col_args, False)
 
 
-def order_kernel(cb, width, pts, slot_ref, first_out, last_out, index):
+def order_kernel(cb, width, adj, pts, slot_ref, adj_out, first_out, last_out, sem):
     levels, rim_blk = first_out.shape
+    half = levels // 2
     span = ZONE * cb
     blocks = pts.shape[1] // LANES
-    index[...] = jnp.zeros(index.shape, jnp.int32)
-    index[:, :rim_blk] = jnp.broadcast_to(slot_ref[...], (2 * levels, rim_blk))
+    carry = pltpu.make_async_copy(adj, adj_out.at[0], sem)
+    carry.start()
     for s in range(0, rim_blk, LANES):
-        q = index[:, s:s + LANES]
+        size = min(LANES, rim_blk - s)
+        q = jnp.broadcast_to(slot_ref[s:s + size].reshape(1, size), (2 * levels, size))
+        if size < LANES:
+            q = jnp.concatenate([q, jnp.zeros((2 * levels, LANES - size), jnp.int32)], axis=1)
         place = jnp.where(q < span, q, jnp.where(q < 2 * span, q + (width - span),
                                                  q + 2 * (width - span)))
         high, low = place // LANES, place % LANES
@@ -280,9 +315,12 @@
         for b in range(blocks):
             found = jnp.take_along_axis(pts[:, b * LANES:(b + 1) * LANES], low, axis=1)
             total = jnp.where(high == b, found, total)
-        size = min(LANES, rim_blk - s)
-        first_out[:, s:s + size] = total[:levels, :size]
-        last_out[:, s:s + size] = total[levels:, :size]
+        total = total[:, :size]
+        first_out[:half, s:s + size] = total[:half]
+        last_out[:half, s:s + size] = total[half:levels]
+        first_out[half:, s:s + size] = total[levels:levels + half]
+        last_out[half:, s:s + size] = total[levels + half:]
+    carry.wait()
 
 
 def body(adj_final, wind_east, wind_north, relax_weight, rim_slot):
@@ -295,42 +333,44 @@
     field = pltpu.VMEM((levels, tile_r, tile_c), f32)
     dma = pltpu.SemaphoreType.DMA
     vmem, anywhere = pl.BlockSpec(memory_space=pltpu.VMEM), pl.BlockSpec(memory_space=pl.ANY)
+    hbm = pl.BlockSpec(memory_space=pltpu.HBM)
     total = 2 * width + LANES
     adj, pts = pl.pallas_call(
         functools.partial(adjoint_kernel, tile_rows, cb),
         out_shape=(jax.ShapeDtypeStruct((levels, tile_r, tile_c), f32),
                    jax.ShapeDtypeStruct((2 * levels, total), f32)),
-        in_specs=[anywhere] * 3 + [pl.BlockSpec(memory_space=pltpu.SMEM)],
+        in_specs=[hbm] * 4,
         out_specs=(vmem, vmem),
         scratch_shapes=[
+            pltpu.SMEM(relax_weight.shape, f32),
             field, field, field, field, field,
             pltpu.VMEM((STEPS, 2, tile_r, LANES), f32),
             pltpu.VMEM((STEPS, 2, tile_r, LANES), f32),
             pltpu.VMEM((STEPS, 2, levels, tile_c), f32),
             pltpu.VMEM((STEPS, 2, levels, tile_c), f32),
+            pltpu.VMEM((levels // 2, 8, LANES), f32),
             pltpu.VMEM((8, levels, LANES), f32),
             pltpu.VMEM((tile_rows, 2 * levels, width), f32),
             pltpu.VMEM((COL_TILES, 2 * levels, LANES), f32),
             pltpu.VMEM((2, 2 * levels, width), f32),
             pltpu.VMEM((2, 2 * levels, LANES), f32),
-            dma((3,)), dma((STEPS, 4)), dma((STEPS, 4)),
+            dma, dma((3,)), dma((STEPS, 4)), dma((STEPS, 4)),
             dma((tile_rows,)), dma((2,)), dma((COL_TILES,)), dma((2,)),
         ],
         compiler_params=pltpu.CompilerParams(
-            collective_id=0, has_side_effects=True, vmem_limit_bytes=32 * 1024 * 1024),
+            collective_id=0, has_side_effects=True),
         cost_estimate=pl.CostEstimate(flops=10_000_000, bytes_accessed=2_200_000,
                                       transcendentals=0),
     )(adj_final, wind_east, wind_north, relax_weight)
-    rim_blk = rim_slot.shape[0]
-    padded = -(-rim_blk // LANES) * LANES
-    first, last = pl.pallas_call(
+    rim = jax.ShapeDtypeStruct((levels, rim_slot.shape[0]), f32)
+    return pl.pallas_call(
         functools.partial(order_kernel, cb, width),
-        out_shape=(jax.ShapeDtypeStruct((levels, rim_blk), f32),) * 2,
-        in_specs=[vmem, vmem],
-        out_specs=(vmem, vmem),
-        scratch_shapes=[pltpu.VMEM((2 * levels, padded), jnp.int32)],
-    )(pts, rim_slot.reshape(1, rim_blk))
-    return (adj[None], first, last)
+        out_shape=(jax.ShapeDtypeStruct((1, levels, tile_r, tile_c), f32), rim, rim),
+        in_specs=[anywhere, vmem, vmem],
+        out_specs=(hbm, vmem, vmem),
+        scratch_shapes=[dma],
+        compiler_params=pltpu.CompilerParams(vmem_limit_bytes=8 * 1024 * 1024),
+    )(adj, pts, rim_slot)
 
 
 def solution(mesh):

time: 22.9 us -> 17.1 us (0.75)
  local copies, waits for them, and re-layouts: 5.82 us -> 1.93 us
  Pallas kernels: 16.2 us -> 14.3 us
    unnamed x13 -> x6, local copies, waits for them, and re-layouts: 5.23 us -> 1.93 us
    pallas_call x1, Pallas kernels: 14 us -> 12.8 us  [body(): pl.pallas_call(functools.partial(adjoint_kernel, tile_rows, cb), out_shap...]
    pallas_call x1, Pallas kernels: 2.1 us -> 1.44 us  [body(): pl.pallas_call(functools.partial(order_kernel, cb, width), out_shape=(jax...]
    reshape x1 -> x0, local copies, waits for them, and re-layouts: 0.59 us -> none  [body(): rim_slot.reshape(1, rim_blk)]
where the time goes in v2:
time: 17.1 us; the launch traced here: 16.9 us
  Pallas kernels  14.3 us (84%)
  local copies, waits for them, and re-layouts  1.93 us (11%)
  between operations  0.66 us (4%)
    pallas_call x1, Pallas kernels, body(): pl.pallas_call(functools.partial(adjoint_kernel, tile_rows, cb), out_shap...  12.8 us
    unnamed x6, local copies, waits for them, and re-layouts  1.93 us
    pallas_call x1, Pallas kernels, body(): pl.pallas_call(functools.partial(order_kernel, cb, width), out_shape=(jax...  1.44 us

profile of v2, /device:TPU:0, one launch (start us, length us, event | category | flops | bytes accessed | tf_op | source)
XLA Modules:
  0.0 16.9 jit_solution(17919917474346042518)
XLA Ops:
  0.6 0.0 copy-start.2
  0.6 12.8 %shard_map.76 = (f32[8,64,256]{2,1,0:T(8,128)}, f32[16,1408]{1,0:T(8,128)}) custom-call(f32[1,8,64,256]{3,2,1,0:T(8,128)} %z_hbm.1, f32[1,8,64,256]{3,2,1,0:T(8,128)} %e_hbm.1, f32[1,8,64,256]{3,2,1,0:T(8,128)} %n_hbm.1, f32[4,8]{1,0:T(4,128)} %relax_hbm.1), custom_call_target="tpu_custom_call" | custom-call | flops 10000000 | bytes 2200000 | tf_op jit(solution)/shard_map/pallas_call | solution.py:338
  13.5 0.0 copy-done.2
  13.5 0.0 copy-start
  13.5 1.0 %copy-done = f32[8,64,256]{2,1,0:T(8,128)S(1)} copy-done((f32[8,64,256]{2,1,0:T(8,128)S(1)}, f32[8,64,256]{2,1,0:T(8,128)}, u32[]{:S(2)}) %copy-start) | copy-done | bytes 524312
  14.5 0.0 copy-start.1
  14.5 0.9 %copy-done.1 = f32[16,1408]{1,0:T(8,128)S(1)} copy-done((f32[16,1408]{1,0:T(8,128)S(1)}, f32[16,1408]{1,0:T(8,128)}, u32[]{:S(2)}) %copy-start.1) | copy-done | bytes 90136
  15.4 1.4 %shard_map.77 = (f32[1,8,64,256]{3,2,1,0:T(8,128)}, f32[8,1360]{1,0:T(8,128)}, f32[8,1360]{1,0:T(8,128)}) custom-call(f32[8,64,256]{2,1,0:T(8,128)S(1)} %copy-done, f32[16,1408]{1,0:T(8,128)S(1)} %copy-done.1, s32[1360]{0:T(1024)S(1)} %copy-done.2), custom_call_target="tpu_custom_call" | custom-call | tf_op jit(solution)/shard_map/pallas_call | solution.py:366
Async XLA Ops:
  0.6 12.8 %copy-start.2 = (s32[1360]{0:T(1024)S(1)}, s32[1360]{0:T(1024)}, u32[]{:S(2)}) copy-start(s32[1360]{0:T(1024)} %slot_ref.1) | copy-start | bytes 16324
  13.5 1.0 %copy-start = (f32[8,64,256]{2,1,0:T(8,128)S(1)}, f32[8,64,256]{2,1,0:T(8,128)}, u32[]{:S(2)}) copy-start(f32[8,64,256]{2,1,0:T(8,128)} %get-tuple-element.5.adj) | copy-start | bytes 1572868
  14.5 0.9 %copy-start.1 = (f32[16,1408]{1,0:T(8,128)S(1)}, f32[16,1408]{1,0:T(8,128)}, u32[]{:S(2)}) copy-start(f32[16,1408]{1,0:T(8,128)} %get-tuple-element.6.pts) | copy-start | bytes 270340

commit v3 on v2

--- a/solution.py
+++ b/solution.py
@@ -358,10 +358,11 @@
             dma((tile_rows,)), dma((2,)), dma((COL_TILES,)), dma((2,)),
         ],
         compiler_params=pltpu.CompilerParams(
-            collective_id=0, has_side_effects=True),
+            collective_id=0, has_side_effects=True, vmem_limit_bytes=32 * 1024 * 1024),
         cost_estimate=pl.CostEstimate(flops=10_000_000, bytes_accessed=2_200_000,
                                       transcendentals=0),
-    )(adj_final, wind_east, wind_north, relax_weight)
+    )(*(pltpu.with_memory_space_constraint(x, pltpu.HBM)
+        for x in (adj_final, wind_east, wind_north, relax_weight)))
     rim = jax.ShapeDtypeStruct((levels, rim_slot.shape[0]), f32)
     return pl.pallas_call(
         functools.partial(order_kernel, cb, width),

time: 17.1 us -> 14.2 us (0.83)
  local copies, waits for them, and re-layouts: 1.93 us -> 0.01 us
  Pallas kernels: 14.3 us -> 13.4 us
    unnamed x6 -> x2, local copies, waits for them, and re-layouts: 1.93 us -> 0.01 us
    pallas_call x1, Pallas kernels: 12.8 us -> 12 us  [body(): pl.pallas_call(functools.partial(adjoint_kernel, tile_rows, cb), out_shap...]
where the time goes in v3:
time: 14.2 us; the launch traced here: 14.1 us
  Pallas kernels  13.4 us (94%)
  between operations  0.66 us (5%)
    pallas_call x1, Pallas kernels, body(): pl.pallas_call(functools.partial(adjoint_kernel, tile_rows, cb), out_shap...  12 us
    pallas_call x1, Pallas kernels, body(): pl.pallas_call(functools.partial(order_kernel, cb, width), out_shape=(jax...  1.44 us

profile of v3, /device:TPU:0, one launch (start us, length us, event | category | flops | bytes accessed | tf_op | source)
XLA Modules:
  0.0 14.1 jit_solution(13031424309773915890)
XLA Ops:
  0.6 0.0 copy-start
  0.6 12.0 %shard_map.76 = (f32[8,64,256]{2,1,0:T(8,128)S(1)}, f32[16,1408]{1,0:T(8,128)S(1)}) custom-call(f32[1,8,64,256]{3,2,1,0:T(8,128)} %z_hbm.1, f32[1,8,64,256]{3,2,1,0:T(8,128)} %e_hbm.1, f32[1,8,64,256]{3,2,1,0:T(8,128)} %n_hbm.1, f32[4,8]{1,0:T(4,128)} %relax_hbm.1), custom_call_target="tpu_custom_call" | custom-call | flops 10000000 | bytes 2200000 | tf_op jit(solution)/shard_map/pallas_call | solution.py:338
  12.6 0.0 copy-done
  12.7 1.4 %shard_map.77 = (f32[1,8,64,256]{3,2,1,0:T(8,128)}, f32[8,1360]{1,0:T(8,128)}, f32[8,1360]{1,0:T(8,128)}) custom-call(f32[8,64,256]{2,1,0:T(8,128)S(1)} %get-tuple-element.5.adj, f32[16,1408]{1,0:T(8,128)S(1)} %get-tuple-element.6.pts, s32[1360]{0:T(1024)S(1)} %copy-done), custom_call_target="tpu_custom_call" | custom-call | tf_op jit(solution)/shard_map/pallas_call | solution.py:367
Async XLA Ops:
  0.6 12.0 %copy-start = (s32[1360]{0:T(1024)S(1)}, s32[1360]{0:T(1024)}, u32[]{:S(2)}) copy-start(s32[1360]{0:T(1024)} %slot_ref.1) | copy-start | bytes 16324
